TPU v7x, 128 devices: a whole 4x4x4 slice. The times are simulated.
128 devices in a mesh: lat: 16 (over y, z_lo, core), lon: 8 (over x, z_hi).
Axes of the slice: x: 4, y: 4, z: 4 (z_hi: 2, z_lo: 2; z = z_hi * 2 + z_lo), core: 2. Of those that a mesh axis runs over, the one named last changes fastest.
Arguments:
- patches: bfloat16 [4, 192, 96, 512], P(None, 'lat', 'lon'), may hold values from -6 to 6
- w_query: bfloat16 [512, 512], replicated, may hold values from -5 to 5
- w_keyval: bfloat16 [512, 1024], replicated, may hold values from -5 to 5
- w_out: bfloat16 [512, 512], replicated, may hold values from -0.25 to 0.25
- w_up: bfloat16 [512, 2048], replicated, may hold values from -0.25 to 0.25
- w_down: bfloat16 [2048, 512], replicated, may hold values from -0.125 to 0.125
- w_merge: bfloat16 [2048, 1024], replicated, may hold values from -0.125 to 0.125
- gain_attn: float32 [512], replicated, may hold values from 0.1 to 1.9
- gain_mlp: float32 [512], replicated, may hold values from 0.1 to 1.9
- gain_merge: float32 [2048], replicated, may hold values from 0.1 to 1.9
- lat_valid: int32 [192], replicated, may hold values 0 or 1
- region_ids: int32 [192], replicated, may hold values from 0 to 24, as said below
Outputs:
- merged: bfloat16 [4, 96, 48, 1024], P(None, 'lat', 'lon')
Inputs may be any that keep to these rules, and one draw needn't show every extreme that they name: `region_ids`: region ids never fall along latitude, start at 0 and rise by one at exactly 24 rows; no rise lies at rows 91 to 102.
All inputs are finite; a program needn't handle non-finite values.
Results may differ from a plain program's by a relative error of at most 0.012.
Values may be sent and summed in bfloat16 or wider, within the bound.
A program may use at most 192 MiB of HBM per device.

v0:
```python
import functools
import math

import jax
import jax.numpy as jnp
import numpy as np
from jax import lax
from jax.experimental import pallas as pl
from jax.experimental.pallas import tpu as pltpu
from jax.sharding import PartitionSpec as P

HEADS = 16
D = 512
FFN = 2048
MERGED = 1024
WIN_LAT = 12
SHIFT_LAT = 6
EPSILON = 1e-05
MESH = pl.DeviceIdType.MESH
F32 = jnp.float32
BF16 = jnp.bfloat16

CELLS = 288
WINDOW = 144
LEVEL_SLOTS = (1, 2, 3, 0)
MERGE_COLS = (((2, 3, 4), (1, 2, 3)), ((5, 0, 1), (4, 5, 0)))


def permutations():
    result = []
    for g in range(2):
        from_win = np.zeros((CELLS, CELLS), np.float32)
        to_final = np.zeros((CELLS, CELLS), np.float32)
        flat_final = np.zeros((CELLS, 576), np.float32)
        for slot, lev in enumerate(LEVEL_SLOTS):
            for wr in range(12):
                for wc in range(6):
                    win = slot * 72 + wr * 6 + wc
                    if g == 0:
                        seg = (wr // 6) * 144 + slot * 36 + (wr % 6) * 6 + wc
                    else:
                        part = wr // 6 + 2 * (wc // 3)
                        seg = part * 72 + slot * 18 + (wr % 6) * 3 + wc % 3
                    row, col = (wr + 6) % 12, (wc + 3 + 6 * g) % 12
                    pos = row % 2 + 2 * (col % 2)
                    jslot = MERGE_COLS[g][col % 2].index(col // 2)
                    final = pos * 72 + jslot * 24 + (row // 2) * 4 + lev
                    from_win[seg, win] = 1
                    to_final[final, seg] = 1
                    flat_final[final, (row * 12 + col) * 4 + lev] = 1
        result += [from_win, to_final, flat_final]
    return [m.astype(jnp.bfloat16) for m in result]


def norm(wide, gain, width):
    average = jnp.sum(wide, axis=-1, keepdims=True) * (1.0 / width)
    centred = wide - average
    variance = jnp.sum(centred * centred, axis=-1, keepdims=True) * (1.0 / width)
    return centred * lax.rsqrt(variance + EPSILON) * gain


def dot(a, b):
    return jnp.dot(a, b, preferred_element_type=F32)


def kernel(
    lat_count,
    lon_count,
    x_hbm, wq_hbm, wkv_hbm, wo_hbm, wup_hbm, wdn_hbm, wm_hbm,
    fromwin0_hbm, tofinal0_hbm, flat0_hbm, fromwin1_hbm, tofinal1_hbm, flat1_hbm,
    ga_hbm, gm_hbm, gg_hbm, valid_hbm, region_hbm,
    out_ref,
    x_v, wq, wkv, wo, wup, wdn, wm,
    fromwin0, tofinal0, flat0, fromwin1, tofinal1, flat1,
    ga_ref, gm_ref, gg_ref, valid_ref, region_ref,
    cells0, cells1, back0, back1, home0, home1, wide, qkv, att, bias, resid, joined,
    local_sem, send_sem, recv_sem,
):
    a, o = lax.axis_index("lat"), lax.axis_index("lon")
    lat_dn = lax.rem(a + lat_count - 1, lat_count)
    lat_up = lax.rem(a + 1, lat_count)
    lon_dn = lax.rem(o + lon_count - 1, lon_count)
    lon_up = lax.rem(o + 1, lon_count)
    lower = ((lat_dn, o), (a, lon_dn), (lat_dn, lon_dn))
    upper = ((lat_up, o), (a, lon_up), (lat_up, lon_up))
    cells, tofinal, flat = (cells0, cells1), (tofinal0, tofinal1), (flat0, flat1)

    barrier = pltpu.get_barrier_semaphore()
    for device in upper:
        pl.semaphore_signal(barrier, inc=1, device_id=device, device_id_type=MESH)

    pairs = (
        (x_hbm.at[pl.ds(6, 6), pl.ds(3, 6)], cells0.at[pl.ds(0, 6)]),
        (x_hbm.at[pl.ds(6, 6), pl.ds(9, 3)], cells1.at[pl.ds(0, 6), pl.ds(0, 3)]),
        (x_hbm, x_v), (wq_hbm, wq), (wkv_hbm, wkv), (flat0_hbm, flat0), (flat1_hbm, flat1),
        (fromwin0_hbm, fromwin0), (fromwin1_hbm, fromwin1),
        (tofinal0_hbm, tofinal0), (tofinal1_hbm, tofinal1),
        (wo_hbm, wo), (wup_hbm, wup), (wdn_hbm, wdn), (wm_hbm, wm),
        (region_hbm, region_ref), (valid_hbm, valid_ref),
        (ga_hbm, ga_ref), (gm_hbm, gm_ref), (gg_hbm, gg_ref),
    )
    loads = [pltpu.make_async_copy(s, d, local_sem.at[i]) for i, (s, d) in enumerate(pairs)]

    def remote(slot, source, target, device):
        return pltpu.make_async_remote_copy(
            src_ref=source, dst_ref=target, send_sem=send_sem.at[slot], recv_sem=recv_sem.at[slot],
            device_id=device, device_id_type=MESH,
        )

    first = [
        remote(0, x_hbm.at[pl.ds(0, 6), pl.ds(3, 6)], cells0.at[pl.ds(6, 6)], lower[0]),
        remote(1, x_hbm.at[pl.ds(0, 6), pl.ds(0, 3)], cells1.at[pl.ds(6, 6), pl.ds(3, 3)], lower[2]),
        remote(2, x_hbm.at[pl.ds(6, 6), pl.ds(0, 3)], cells1.at[pl.ds(0, 6), pl.ds(3, 3)], lower[1]),
        remote(3, x_hbm.at[pl.ds(0, 6), pl.ds(9, 3)], cells1.at[pl.ds(6, 6), pl.ds(0, 3)], lower[0]),
    ]
    for load in loads[15:17] + loads[:3]:
        load.start()
    pl.semaphore_wait(barrier, 3)
    for copy in first:
        copy.start()
    for load in loads[17:] + loads[3:15]:
        load.start()

    key_row = lax.broadcasted_iota(jnp.int32, (WINDOW, 128), 0)
    key_lev = (key_row >= 72).astype(jnp.int32)
    key_lat = ((key_row - 72 * key_lev) * 683) >> 12
    start = a * WIN_LAT + SHIFT_LAT
    loads[15].wait()
    loads[16].wait()
    row_ids = [lax.rem(start + r, lat_count * WIN_LAT) for r in range(WIN_LAT)]
    tags = [region_ref[i] for i in row_ids]
    valid = [valid_ref[i] for i in row_ids]
    key_tag = jnp.zeros((WINDOW, 128), jnp.int32)
    key_valid = jnp.zeros((WINDOW, 128), jnp.int32)
    for r in range(WIN_LAT):
        key_tag = jnp.where(key_lat == r, tags[r], key_tag)
        key_valid = jnp.where(key_lat == r, valid[r], key_valid)
    lane = lax.broadcasted_iota(jnp.int32, (1, 128), 1) & 15
    for b in range(9):
        query = lane + 16 * b
        query_lev = (query >= 72).astype(jnp.int32)
        query_lat = ((query - 72 * query_lev) * 683) >> 12
        query_tag = jnp.zeros((1, 128), jnp.int32)
        for r in range(WIN_LAT):
            query_tag = jnp.where(query_lat == r, tags[r], query_tag)
        usable = (key_tag == query_tag) & ((key_valid == 1) | (key_row == query))
        bias[0, b] = jnp.where(usable, 0.0, -jnp.inf)
        bias[1, b] = jnp.where(usable & (key_lev == query_lev), 0.0, -jnp.inf)

    first[0].wait_send()

    for i in (2, 5, 6, 17):
        loads[i].wait()
    mine = jnp.concatenate([x_v[r].astype(F32).reshape(48, D) for r in range(12)], axis=0).astype(BF16)
    for g in range(2):
        resid[g] = dot(flat[g][...], mine)

    head_lane = lax.broadcasted_iota(jnp.int32, (16, 256), 1) >> 5
    head_mask = [(head_lane == h).astype(F32).astype(BF16) for h in range(8)]
    factor = math.log2(math.e) / math.sqrt(D // HEADS)

    second = []
    for g in range(2):
        loads[g].wait()
        for copy in (first[:1], first[1:])[g]:
            copy.wait_recv()
        if g == 0:
            loads[3].wait()
            loads[4].wait()
        for row in range(12):
            flat_row = cells[g][row].astype(F32).reshape(24, D)
            for c in range(4):
                wide[c, 24 * row : 24 * row + 24, :] = flat_row[:, 128 * c : 128 * c + 128]
        levels = [
            jnp.concatenate([wide[c, pl.ds(lev, 72, stride=4), :] for c in range(4)], axis=1)
            for lev in LEVEL_SLOTS
        ]
        normed = norm(jnp.concatenate(levels, axis=0), ga_ref[...], D).astype(BF16)
        qkv[:, 0:D] = dot(normed, wq[...]).astype(BF16)
        qkv[:, D : 3 * D] = dot(normed, wkv[...]).astype(BF16)

        def attend(half):
            col0 = half * 256
            units = [(window, b) for window in range(2) for b in range(9)]
            scores, weights, heads = {}, {}, {}
            for window, b in units:
                row0 = window * WINDOW
                keys = qkv[row0 : row0 + WINDOW, D + col0 : D + col0 + 256]
                query = qkv[row0 + 16 * b : row0 + 16 * b + 16, col0 : col0 + 256]
                spread = jnp.concatenate([query * m for m in head_mask], axis=0)
                scores[window, b] = lax.dot_general(
                    keys, spread, (((1,), (1,)), ((), ())), preferred_element_type=F32
                )
            for window, b in units:
                logits = scores[window, b] * factor + bias[window, b]
                top = jnp.max(logits, axis=0, keepdims=True)
                raised = jnp.exp2(logits - top)
                total = jnp.sum(raised, axis=0, keepdims=True)
                weights[window, b] = (raised * (1.0 / total)).astype(BF16)
            for window, b in units:
                row0 = window * WINDOW
                values = qkv[row0 : row0 + WINDOW, 2 * D + col0 : 2 * D + col0 + 256]
                heads[window, b] = lax.dot_general(
                    weights[window, b], values, (((0,), (0,)), ((), ())), preferred_element_type=F32
                )
            for window, b in units:
                picked = jnp.zeros((16, 256), F32)
                for h in range(8):
                    picked = jnp.where(head_lane == h, heads[window, b][16 * h : 16 * h + 16], picked)
                at = window * WINDOW + 16 * b
                att[at : at + 16, col0 : col0 + 256] = picked.astype(BF16)

        loads[7 + g].wait()
        second.append([])
        if g == 0:
            for half in range(2):
                attend(half)
            back0[...] = dot(fromwin0[...], att[...]).astype(BF16)
            part = pl.ds(144, 144)
            second[0].append(remote(4, back0.at[part], home0.at[part], upper[0]))
            second[0][0].start()
        else:
            for half in range(2):
                attend(half)
                moved = dot(fromwin1[...], att[:, 256 * half : 256 * half + 256])
                back1[half] = moved.reshape(36, 8, 256).astype(BF16)
                for i in (2, 1, 0):
                    part = (half, pl.ds(9 * i + 9, 9))
                    copy = remote(5 + 3 * half + i, back1.at[part], home1.at[part], upper[i])
                    copy.start()
                    second[1].append(copy)

    for i in (9, 10, 11, 12, 13, 14, 18, 19):
        loads[i].wait()

    for g in range(2):
        if g == 0:
            second[0][0].wait_recv()
            staged = jnp.concatenate([back0[0:144], home0[144:288]], axis=0)
            attended = dot(tofinal[0][...], staged).astype(BF16)
            after = (resid[0] + dot(attended, wo[...])).astype(BF16)
        else:
            after = resid[1]
            for half in range(2):
                for copy in second[1][3 * half : 3 * half + 3]:
                    copy.wait_recv()
                tiles = jnp.concatenate([back1[half, 0:9], home1[half, 9:36]], axis=0)
                staged = tiles.astype(F32).reshape(CELLS, 256).astype(BF16)
                attended = dot(tofinal[1][...], staged).astype(BF16)
                after = after + dot(attended, wo[256 * half : 256 * half + 256, :])
            after = after.astype(BF16)
        after_wide = after.astype(F32)
        normed = norm(after_wide, gm_ref[...], D).astype(BF16)
        total = after_wide
        for c in range(2):
            cols = slice(c * 1024, c * 1024 + 1024)
            up = dot(normed, wup[:, cols])
            hidden = (0.5 * up * (1.0 + lax.erf(up * (2.0 ** -0.5)))).astype(BF16)
            total = total + dot(hidden, wdn[cols, :])
        done = total.astype(BF16).astype(F32)
        for pos in range(4):
            for jslot, j in enumerate(MERGE_COLS[g][pos // 2]):
                at = pos * 72 + jslot * 24
                joined[24 * j : 24 * j + 24, D * pos : D * pos + D] = done[at : at + 24]
    merged = dot(norm(joined[...], gg_ref[...], 4 * D).astype(BF16), wm[...])
    for j in range(6):
        tiles = merged[24 * j : 24 * j + 24].reshape(6, 4, MERGED).astype(BF16)
        for i in range(6):
            out_ref[i, j] = tiles[i]

    for copy in first[1:] + second[0] + second[1]:
        copy.wait_send()


def on_device(
    lat_count, lon_count, patches, w_query, w_keyval, w_out, w_up, w_down, w_merge,
    gain_attn, gain_mlp, gain_merge, lat_valid, region_ids,
):
    perms = [jnp.asarray(m) for m in permutations()]
    hbm = pl.BlockSpec(memory_space=pl.ANY)
    vmem = pl.BlockSpec(memory_space=pltpu.VMEM)
    grid = patches.transpose(1, 2, 0, 3)
    weights = (w_query, w_keyval, w_out, w_up, w_down, w_merge)
    held = [pltpu.VMEM(v.shape, v.dtype) for v in (grid,) + weights + tuple(perms)]
    merged = pl.pallas_call(
        functools.partial(kernel, lat_count, lon_count),
        out_shape=pltpu.VMEM((6, 6, 4, MERGED), BF16),
        in_specs=[hbm] * 18,
        out_specs=vmem,
        scratch_shapes=held
        + [
            pltpu.VMEM((1, D), F32),
            pltpu.VMEM((1, D), F32),
            pltpu.VMEM((1, 4 * D), F32),
            pltpu.SMEM(lat_valid.shape, jnp.int32),
            pltpu.SMEM(region_ids.shape, jnp.int32),
            pltpu.VMEM((12, 6, 4, D), BF16),
            pltpu.VMEM((12, 6, 4, D), BF16),
            pltpu.VMEM((CELLS, D), BF16),
            pltpu.VMEM((2, 36, 8, 256), BF16),
            pltpu.VMEM((CELLS, D), BF16),
            pltpu.VMEM((2, 36, 8, 256), BF16),
            pltpu.VMEM((4, CELLS, 128), F32),
            pltpu.VMEM((CELLS, 3 * D), BF16),
            pltpu.VMEM((CELLS, D), BF16),
            pltpu.VMEM((2, 9, WINDOW, 128), F32),
            pltpu.VMEM((2, CELLS, D), F32),
            pltpu.VMEM((144, 4 * D), F32),
            pltpu.SemaphoreType.DMA((20,)),
            pltpu.SemaphoreType.DMA((11,)),
            pltpu.SemaphoreType.DMA((11,)),
        ],
        compiler_params=pltpu.CompilerParams(
            collective_id=0, has_side_effects=True, vmem_limit_bytes=56 * 1024 * 1024
        ),
        cost_estimate=pl.CostEstimate(
            flops=6_000_000_000, bytes_accessed=12_000_000, transcendentals=3_000_000
        ),
    )(
        grid, *weights, *perms,
        gain_attn.reshape(1, -1), gain_mlp.reshape(1, -1), gain_merge.reshape(1, -1),
        lat_valid, region_ids,
    )
    return merged.transpose(2, 0, 1, 3)


def solution(mesh):
    placed = (P(None, "lat", "lon", None),) + (P(),) * 11
    return jax.shard_map(
        functools.partial(on_device, mesh.shape["lat"], mesh.shape["lon"]),
        mesh=mesh,
        in_specs=placed,
        out_specs=P(None, "lat", "lon", None),
        check_vma=False,
    )
```

profile of v0, /device:TPU:0, one launch (start us, length us, event | category | flops | bytes accessed | tf_op | source)
XLA Modules:
  0.0 28.1 jit_solution(13635733493289027929)
XLA Ops:
  0.0 27.4 %shard_map.172 = bf16[6,6,4,1024]{3,2,1,0:T(4,128)(2,1)S(1)} custom-call(bf16[12,12,4,512]{3,2,1,0:T(4,128)(2,1)} %bitcast.6, bf16[512,512]{1,0:T(8,128)(2,1)} %wq_hbm.1, bf16[512,1024]{1,0:T(8,128)(2,1)} %wkv_hbm.1, bf16[512,512]{1,0:T(8,128)(2,1)} %wo_hbm.1, bf16[512,2048]{1,0:T(8,128)(2,1)} %wup_hbm.1, bf16[2048,512]{1,0:T(8,128)(2,1)} %wdn_hbm.1, ...), custom_call_target="tpu_custom_call" | custom-call | flops 6000000000 | bytes 12000000 | tf_op jit(solution)/shard_map/pallas_call | solution.py:285
  27.4 0.7 %copy.20 = bf16[4,6,6,1024]{3,0,2,1:T(4,128)(2,1)} copy(bf16[4,6,6,1024]{3,0,2,1:T(4,128)(2,1)S(1)} %bitcast.5) | data formatting | bytes 589824
where the time goes:
time: 28.2 us; the launch traced here: 28.1 us
  Pallas kernels  27.4 us (97%)
  local copies, waits for them, and re-layouts  0.72 us (3%)
    pallas_call x1, Pallas kernels, on_device(): pl.pallas_call(functools.partial(kernel, lat_count, lon_count), out_shape...  27.4 us
    unnamed x1, local copies, waits for them, and re-layouts  0.72 us

commit v1 on v0

--- a/solution.py
+++ b/solution.py
@@ -215,10 +215,11 @@
         if g == 0:
             for half in range(2):
                 attend(half)
-            back0[...] = dot(fromwin0[...], att[...]).astype(BF16)
-            part = pl.ds(144, 144)
-            second[0].append(remote(4, back0.at[part], home0.at[part], upper[0]))
-            second[0][0].start()
+                moved = dot(fromwin0[...], att[:, 256 * half : 256 * half + 256])
+                back0[half] = moved.astype(BF16)
+                part = (half, pl.ds(144, 144))
+                second[0].append(remote((4, 11)[half], back0.at[part], home0.at[part], upper[0]))
+                second[0][half].start()
         else:
             for half in range(2):
                 attend(half)
@@ -235,8 +236,10 @@
 
     for g in range(2):
         if g == 0:
-            second[0][0].wait_recv()
-            staged = jnp.concatenate([back0[0:144], home0[144:288]], axis=0)
+            for copy in second[0]:
+                copy.wait_recv()
+            parts = [jnp.concatenate([back0[h, 0:144], home0[h, 144:288]], axis=0) for h in range(2)]
+            staged = jnp.concatenate(parts, axis=1)
             attended = dot(tofinal[0][...], staged).astype(BF16)
             after = (resid[0] + dot(attended, wo[...])).astype(BF16)
         else:
@@ -296,9 +299,9 @@
             pltpu.SMEM(region_ids.shape, jnp.int32),
             pltpu.VMEM((12, 6, 4, D), BF16),
             pltpu.VMEM((12, 6, 4, D), BF16),
-            pltpu.VMEM((CELLS, D), BF16),
+            pltpu.VMEM((2, CELLS, 256), BF16),
             pltpu.VMEM((2, 36, 8, 256), BF16),
-            pltpu.VMEM((CELLS, D), BF16),
+            pltpu.VMEM((2, CELLS, 256), BF16),
             pltpu.VMEM((2, 36, 8, 256), BF16),
             pltpu.VMEM((4, CELLS, 128), F32),
             pltpu.VMEM((CELLS, 3 * D), BF16),
@@ -307,8 +310,8 @@
             pltpu.VMEM((2, CELLS, D), F32),
             pltpu.VMEM((144, 4 * D), F32),
             pltpu.SemaphoreType.DMA((20,)),
-            pltpu.SemaphoreType.DMA((11,)),
-            pltpu.SemaphoreType.DMA((11,)),
+            pltpu.SemaphoreType.DMA((12,)),
+            pltpu.SemaphoreType.DMA((12,)),
         ],
         compiler_params=pltpu.CompilerParams(
             collective_id=0, has_side_effects=True, vmem_limit_bytes=56 * 1024 * 1024

time: 28.2 us -> 28.3 us (level)
  no operation moved by 1% of the time
where the time goes in v1:
time: 28.3 us; the launch traced here: 28.2 us
  Pallas kernels  27.4 us (97%)
  local copies, waits for them, and re-layouts  0.72 us (3%)
    pallas_call x1, Pallas kernels, on_device(): pl.pallas_call(functools.partial(kernel, lat_count, lon_count), out_shape...  27.4 us
    unnamed x1, local copies, waits for them, and re-layouts  0.72 us

profile of v1, /device:TPU:0, one launch (start us, length us, event | category | flops | bytes accessed | tf_op | source)
XLA Modules:
  0.0 28.2 jit_solution(12482323856120108559)
XLA Ops:
  0.0 27.4 %shard_map.172 = bf16[6,6,4,1024]{3,2,1,0:T(4,128)(2,1)S(1)} custom-call(bf16[12,12,4,512]{3,2,1,0:T(4,128)(2,1)} %bitcast.6, bf16[512,512]{1,0:T(8,128)(2,1)} %wq_hbm.1, bf16[512,1024]{1,0:T(8,128)(2,1)} %wkv_hbm.1, bf16[512,512]{1,0:T(8,128)(2,1)} %wo_hbm.1, bf16[512,2048]{1,0:T(8,128)(2,1)} %wup_hbm.1, bf16[2048,512]{1,0:T(8,128)(2,1)} %wdn_hbm.1, ...), custom_call_target="tpu_custom_call" | custom-call | flops 6000000000 | bytes 12000000 | tf_op jit(solution)/shard_map/pallas_call | solution.py:288
  27.4 0.7 %copy.20 = bf16[4,6,6,1024]{3,0,2,1:T(4,128)(2,1)} copy(bf16[4,6,6,1024]{3,0,2,1:T(4,128)(2,1)S(1)} %bitcast.5) | data formatting | bytes 589824
